TPU v7x, 256 devices: a whole 4x4x8 slice. The times are simulated.
256 devices in a mesh: band: 64 (over z, x, core), tm: 4 (over y).
Axes of the slice: x: 4, y: 4, z: 8, core: 2. Of those that a mesh axis runs over, the one named last changes fastest.
Arguments:
- spectra: float32 [64, 64, 16384], P(None, 'band', 'tm'), may hold values from -6 to 6
- newest: float32 [64, 64, 4, 1024], P(None, 'band', 'tm')
- ingest_owner: int32 [64], P('band'), may hold values from 0 to 3
- low_trial: int32 [4, 4096], P(None, 'band'), may hold values from 0 to 7, as said below
- high_trial: int32 [4, 4096], P(None, 'band'), may hold values from 0 to 7, as said below
- delay_table: int32 [4, 4096], P(None, 'band'), may hold values from 0 to 64, as said below
Outputs:
- dedispersed: float32 [256, 16, 16384], P('band', None, 'tm')
Inputs may be any that keep to these rules, and one draw needn't show every extreme that they name: `low_trial`: at level l (row l-1) entry r belongs to trial r % 2^l and names a trial below 2^(l-1); the highest trial of each subband names trial 2^(l-1) - 1. `high_trial`: as low_trial, for the upper half-subband. `delay_table`: at level l the delays are at most 8 * 2^(l-1), reached by the highest trial of each subband.
All inputs are finite; a program needn't handle non-finite values.
Results may differ from a plain program's by a relative error of at most 0.0003.
Values sent between devices are 32-bit elements; how exact they have to be, the bound alone decides.
A program may use at most 64 MiB of HBM per device.

v0:
```python
import jax
import jax.numpy as jnp
from jax import lax
from jax.sharding import PartitionSpec as P

LEVELS = 4
SHIFT = 8


def spread(value, axis, source):
    kept = jnp.where(lax.axis_index(axis) == source, value, 0).astype(value.dtype)
    return lax.psum(kept, axis)


def from_behind(block, axis, distance):
    devices = range(lax.axis_size(axis))
    route = [(i - distance, i) for i in devices if i - distance in devices]
    return lax.ppermute(block, axis, route)


def channel_stats(ingest):
    block_mean = jnp.mean(ingest, axis=-1)
    centred = ingest - block_mean[:, None]
    inv_scale = 1.0 / jnp.sqrt(jnp.mean(centred * centred, axis=-1) + 1e-06)
    return (block_mean, inv_scale)


def delayed_rows(source, shifts, length):
    reach_max = source.shape[1] - length
    shifted = source
    for bit_pos in range(reach_max.bit_length()):
        step_size = 1 << bit_pos
        moved = jnp.concatenate(
            [jnp.zeros((source.shape[0], step_size), source.dtype), shifted[:, :-step_size]], axis=1
        )
        flags = jnp.right_shift(shifts, bit_pos) % 2 == 1
        shifted = jnp.where(flags[:, None], moved, shifted)
    return shifted[:, reach_max:]


def shards(spectra, newest, ingest_owner, low_trial, high_trial, delay_table):
    ingest = newest[:, 0, 0, :]
    root_slot = ingest_owner[0]
    received = spread(ingest, "tm", root_slot)
    block_mean, inv_scale = channel_stats(received)
    normed = (spectra[:, 0, :] - block_mean[:, None]) * inv_scale[:, None]
    chan_dev, time_dev = normed.shape
    moved = lax.all_to_all(
        normed[:, None, :], "band", split_axis=0, concat_axis=1, tiled=True
    ).reshape(chan_dev, time_dev)
    current = moved
    row_ids = jnp.arange(chan_dev, dtype=jnp.int32)
    for layer_idx in range(LEVELS):
        half_span = 2**layer_idx
        span_width = 2 * half_span
        reach_max = SHIFT * half_span
        low_rows = row_ids // span_width * span_width + low_trial[layer_idx]
        odd_rows = current.reshape(chan_dev // span_width, 2, half_span, time_dev)[:, 1].reshape(
            chan_dev // 2, time_dev
        )
        received_rim = from_behind(odd_rows[:, time_dev - reach_max :], "tm", 1)
        extended = jnp.concatenate([received_rim, odd_rows], axis=1)
        odd_index = row_ids // span_width * half_span + high_trial[layer_idx]
        current = current[low_rows] + delayed_rows(
            extended[odd_index], delay_table[layer_idx], time_dev
        )
    return current.reshape(chan_dev // 2**LEVELS, 2**LEVELS, time_dev)


def solution(mesh):
    return jax.shard_map(
        shards,
        mesh=mesh,
        in_specs=(
            P(None, "band", "tm"),
            P(None, "band", "tm", None),
            P("band"),
            P(None, "band"),
            P(None, "band"),
            P(None, "band"),
        ),
        out_specs=P("band", None, "tm"),
        check_vma=False,
    )
```

profile of v0, /device:TPU:16, one launch (start us, length us, event | category | flops | bytes accessed | tf_op | source)
XLA Modules:
  0.0 148.1 jit_solution(2413679411393339932)
XLA Ops:
  7.5 0.8 copy.18
  8.3 50.2 %all-reduce.24.cloned.1.call-done = f32[64,1024]{1,0:T(8,128)} async-done(((f32[64,1024]{1,0:T(8,128)}), f32[64,1024]{1,0:T(8,128)}) %all-reduce.24.cloned.1.call-update) | async-done | bytes 262160 | tf_op jit(solution)/shard_map/psum | solution.py:12
  58.5 1.1 reduce_sum.18
  59.6 1.2 multiply_reduce_fusion
  60.8 2.4 %subtract_multiply_fusion = f32[64,1,4096]{2,1,0:T(1,128)} fusion(f32[64,1,4096]{2,1,0:T(1,128)S(1)} %copy-done, f32[64]{0:T(128)S(1)} %add_rsqrt_fusion, f32[64]{0:T(128)S(1)} %broadcast_multiply_fusion), kind=kLoop, calls=%fused_computation.35 | loop fusion | flops 524288 | bytes 2097664 | tf_op jit(solution)/shard_map/mul | solution.py:46
  63.2 10.6 %all-to-all-start = ((f32[64,1,4096]{2,1,0:T(1,128)}), f32[64,1,4096]{2,1,0:T(1,128)S(1)}, u32[]{:S(2)}, u32[]{:S(2)}) async-start(f32[64,1,4096]{2,1,0:T(1,128)} %subtract_multiply_fusion), calls=%async_computation | async-start | bytes 2097152 | tf_op jit(solution)/shard_map/all_to_all | solution.py:48
  73.9 28.7 %all-to-all-done = f32[64,1,4096]{2,1,0:T(1,128)S(1)} async-done(((f32[64,1,4096]{2,1,0:T(1,128)}), f32[64,1,4096]{2,1,0:T(1,128)S(1)}, u32[]{:S(2)}, u32[]{:S(2)}) %all-to-all-start) | async-done | bytes 1048608 | tf_op jit(solution)/shard_map/all_to_all | solution.py:48
  103.1 2.8 %collective-permute-start = (f32[32,8]{1,0:T(8,128)S(1)}, f32[32,8]{1,0:T(8,128)S(1)}, u32[]{:S(2)}, u32[]{:S(2)}) collective-permute-start(f32[32,8]{1,0:T(8,128)S(1)} %slice.201), channel_id=1, source_target_pairs={{0,1},{1,2},{2,3},{4,5},{5,6},{6,7},{8,9},{9,10},{10,11},{12,13},{... | collective-permute-start | bytes 3080 | tf_op jit(solution)/shard_map/ppermute | solution.py:18
  105.9 0.6 copy.16
  106.5 0.9 gather_fusion
  107.4 1.3 collective-permute-done
  108.9 1.0 gather_fusion.1
  109.9 0.4 pad_select_fusion.17
  110.6 0.4 pad_select_fusion.15
  111.4 0.6 reshape.749
  112.1 0.4 reshape_squeeze.13
  112.5 2.8 %collective-permute-start.1 = (f32[32,16]{1,0:T(8,128)S(1)}, f32[32,16]{1,0:T(8,128)S(1)}, u32[]{:S(2)}, u32[]{:S(2)}) collective-permute-start(f32[32,16]{1,0:T(8,128)S(1)} %slice.208), channel_id=1, source_target_pairs={{0,1},{1,2},{2,3},{4,5},{5,6},{6,7},{8,9},{9,10},{10,11},{12,13},{... | collective-permute-start | bytes 6152 | tf_op jit(solution)/shard_map/ppermute | solution.py:18
  115.3 0.9 gather_fusion.2
  116.2 1.9 %collective-permute-done.1 = f32[32,16]{1,0:T(8,128)S(1)} collective-permute-done((f32[32,16]{1,0:T(8,128)S(1)}, f32[32,16]{1,0:T(8,128)S(1)}, u32[]{:S(2)}, u32[]{:S(2)}) %collective-permute-start.1) | collective-permute-done | bytes 2080 | tf_op jit(solution)/shard_map/ppermute | solution.py:18
  118.3 1.0 gather_fusion.3
  119.7 0.4 pad_select_fusion.13
  121.8 3.0 %collective-permute-start.2 = (f32[32,32]{1,0:T(8,128)S(1)}, f32[32,32]{1,0:T(8,128)S(1)}, u32[]{:S(2)}, u32[]{:S(2)}) collective-permute-start(f32[32,32]{1,0:T(8,128)S(1)} %slice.216), channel_id=1, source_target_pairs={{0,1},{1,2},{2,3},{4,5},{5,6},{6,7},{8,9},{9,10},{10,11},{12,13},{... | collective-permute-start | bytes 12296 | tf_op jit(solution)/shard_map/ppermute | solution.py:18
  124.8 0.9 gather_fusion.4
  125.7 1.7 %collective-permute-done.2 = f32[32,32]{1,0:T(8,128)S(1)} collective-permute-done((f32[32,32]{1,0:T(8,128)S(1)}, f32[32,32]{1,0:T(8,128)S(1)}, u32[]{:S(2)}, u32[]{:S(2)}) %collective-permute-start.2) | collective-permute-done | bytes 4128 | tf_op jit(solution)/shard_map/ppermute | solution.py:18
  127.6 1.0 gather_fusion.5
  128.9 0.4 pad_select_fusion.9
  129.3 0.4 pad_select_fusion.8
  130.9 2.8 %collective-permute-start.3 = (f32[32,64]{1,0:T(8,128)S(1)}, f32[32,64]{1,0:T(8,128)S(1)}, u32[]{:S(2)}, u32[]{:S(2)}) collective-permute-start(f32[32,64]{1,0:T(8,128)S(1)} %slice.225), channel_id=1, source_target_pairs={{0,1},{1,2},{2,3},{4,5},{5,6},{6,7},{8,9},{9,10},{10,11},{12,13},{... | collective-permute-start | bytes 24584 | tf_op jit(solution)/shard_map/ppermute | solution.py:18
  133.7 0.9 gather_fusion.6
  134.7 1.9 %collective-permute-done.3 = f32[32,64]{1,0:T(8,128)S(1)} collective-permute-done((f32[32,64]{1,0:T(8,128)S(1)}, f32[32,64]{1,0:T(8,128)S(1)}, u32[]{:S(2)}, u32[]{:S(2)}) %collective-permute-start.3) | collective-permute-done | bytes 8224 | tf_op jit(solution)/shard_map/ppermute | solution.py:18
  136.7 1.0 gather_fusion.7
  139.9 1.3 fusion
  (59 shorter events, 8.4 us)
Async XLA Ops:
  6.5 54.2 %copy-start = (f32[64,1,4096]{2,1,0:T(1,128)S(1)}, f32[64,1,4096]{2,1,0:T(1,128)}, u32[]{:S(2)}) copy-start(f32[64,1,4096]{2,1,0:T(1,128)} %param.6) | copy-start | bytes 3145732
  6.5 52.0 %all-reduce.24.cloned.1.call-start = ((), (), s32[]{:S(2)}) async-start(), calls=%async_computation.1 | async-start | bytes 524288 | tf_op jit(solution)/shard_map/psum | solution.py:12
  63.2 10.6 %copy-start.2 = (s32[4,64]{1,0:T(4,128)S(1)}, s32[4,64]{1,0:T(4,128)}, u32[]{:S(2)}) copy-start(s32[4,64]{1,0:T(4,128)} %param.9) | copy-start | bytes 3076
  63.2 10.6 %copy-start.3 = (s32[4,64]{1,0:T(4,128)S(1)}, s32[4,64]{1,0:T(4,128)}, u32[]{:S(2)}) copy-start(s32[4,64]{1,0:T(4,128)} %param.10) | copy-start | bytes 3076
  63.2 10.7 %copy-start.1 = (s32[4,64]{1,0:T(4,128)S(1)}, s32[4,64]{1,0:T(4,128)}, u32[]{:S(2)}) copy-start(s32[4,64]{1,0:T(4,128)} %param.11) | copy-start | bytes 3076
  63.2 39.5 %all-to-all-start = ((f32[64,1,4096]{2,1,0:T(1,128)}), f32[64,1,4096]{2,1,0:T(1,128)S(1)}, u32[]{:S(2)}, u32[]{:S(2)}) async-start(f32[64,1,4096]{2,1,0:T(1,128)} %subtract_multiply_fusion), calls=%async_computation | async-start | bytes 2097152 | tf_op jit(solution)/shard_map/all_to_all | solution.py:48
  103.1 5.6 %collective-permute-start = (f32[32,8]{1,0:T(8,128)S(1)}, f32[32,8]{1,0:T(8,128)S(1)}, u32[]{:S(2)}, u32[]{:S(2)}) collective-permute-start(f32[32,8]{1,0:T(8,128)S(1)} %slice.201), channel_id=1, source_target_pairs={{0,1},{1,2},{2,3},{4,5},{5,6},{6,7},{8,9},{9,10},{10,11},{12,13},{... | collective-permute-start | bytes 3080 | tf_op jit(solution)/shard_map/ppermute | solution.py:18
  112.5 5.6 %collective-permute-start.1 = (f32[32,16]{1,0:T(8,128)S(1)}, f32[32,16]{1,0:T(8,128)S(1)}, u32[]{:S(2)}, u32[]{:S(2)}) collective-permute-start(f32[32,16]{1,0:T(8,128)S(1)} %slice.208), channel_id=1, source_target_pairs={{0,1},{1,2},{2,3},{4,5},{5,6},{6,7},{8,9},{9,10},{10,11},{12,13},{... | collective-permute-start | bytes 6152 | tf_op jit(solution)/shard_map/ppermute | solution.py:18
  121.8 5.6 %collective-permute-start.2 = (f32[32,32]{1,0:T(8,128)S(1)}, f32[32,32]{1,0:T(8,128)S(1)}, u32[]{:S(2)}, u32[]{:S(2)}) collective-permute-start(f32[32,32]{1,0:T(8,128)S(1)} %slice.216), channel_id=1, source_target_pairs={{0,1},{1,2},{2,3},{4,5},{5,6},{6,7},{8,9},{9,10},{10,11},{12,13},{... | collective-permute-start | bytes 12296 | tf_op jit(solution)/shard_map/ppermute | solution.py:18
  130.9 5.6 %collective-permute-start.3 = (f32[32,64]{1,0:T(8,128)S(1)}, f32[32,64]{1,0:T(8,128)S(1)}, u32[]{:S(2)}, u32[]{:S(2)}) collective-permute-start(f32[32,64]{1,0:T(8,128)S(1)} %slice.225), channel_id=1, source_target_pairs={{0,1},{1,2},{2,3},{4,5},{5,6},{6,7},{8,9},{9,10},{10,11},{12,13},{... | collective-permute-start | bytes 24584 | tf_op jit(solution)/shard_map/ppermute | solution.py:18
Sparse Core Ops, SparseCore 0:
  9.7 48.7 all-reduce.23
where the time goes:
time: 148 us
  waiting for transfers between devices  85.7 us (58%)
  starting transfers between devices  21.9 us (15%)
  between operations  14.6 us (10%)
  other arithmetic  14.5 us (10%)
  local copies, waits for them, and re-layouts  11.5 us (8%)
    psum x1, waiting for transfers between devices, spread(): return lax.psum(kept, axis)  50.2 us
    all_to_all x1, waiting for transfers between devices, shards(): lax.all_to_all(normed[:, None, :], 'band', split_axis=0, concat_axis=1, t...  28.7 us
    ppermute x4, starting transfers between devices, from_behind(): return lax.ppermute(block, axis, route)  11.3 us
    all_to_all x1, starting transfers between devices, shards(): lax.all_to_all(normed[:, None, :], 'band', split_axis=0, concat_axis=1, t...  10.6 us
    ppermute x4, waiting for transfers between devices, from_behind(): return lax.ppermute(block, axis, route)  6.74 us
    select_n x18, other arithmetic, delayed_rows(): shifted = jnp.where(flags[:, None], moved, shifted)  6.34 us
    gather x4, local copies, waits for them, and re-layouts, shards(): extended[odd_index]  3.88 us
    gather x4, local copies, waits for them, and re-layouts, shards(): current[low_rows]  3.7 us
  transfers between devices with their start and end apart: 6, of which 6 were waited for; matrix products, arithmetic and copies ran while one was open for 3% of the time, Pallas kernels for 0%

commit v1 on v0

--- a/solution.py
+++ b/solution.py
@@ -9,7 +9,7 @@
 
 def spread(value, axis, source):
     kept = jnp.where(lax.axis_index(axis) == source, value, 0).astype(value.dtype)
-    return lax.psum(kept, axis)
+    return jnp.sum(lax.all_gather(kept, axis_name=axis), axis=0)
 
 
 def from_behind(block, axis, distance):

time: 148 us -> 130 us (0.88)
  waiting for transfers between devices: 85.7 us -> 63.8 us
  local copies, waits for them, and re-layouts: 11.5 us -> 13.3 us
    psum x1 -> x0, waiting for transfers between devices: 50.2 us -> none  [spread(): return lax.psum(kept, axis)]
    all_gather x0 -> x1, waiting for transfers between devices: none -> 29.5 us  [spread(): return jnp.sum(lax.all_gather(kept, axis_name=axis), axis=0)]
    unnamed x11 -> x13, local copies, waits for them, and re-layouts: 1.68 us -> 3.48 us
where the time goes in v1:
time: 130 us; the launch traced here: 129 us
  waiting for transfers between devices  63.8 us (49%)
  starting transfers between devices  23 us (18%)
  between operations  14.5 us (11%)
  other arithmetic  14.4 us (11%)
  local copies, waits for them, and re-layouts  13.3 us (10%)
    all_gather x1, waiting for transfers between devices, spread(): return jnp.sum(lax.all_gather(kept, axis_name=axis), axis=0)  29.5 us
    all_to_all x1, waiting for transfers between devices, shards(): lax.all_to_all(normed[:, None, :], 'band', split_axis=0, concat_axis=1, t...  28.7 us
    ppermute x4, starting transfers between devices, from_behind(): return lax.ppermute(block, axis, route)  12.5 us
    all_to_all x1, starting transfers between devices, shards(): lax.all_to_all(normed[:, None, :], 'band', split_axis=0, concat_axis=1, t...  10.6 us
    select_n x18, other arithmetic, delayed_rows(): shifted = jnp.where(flags[:, None], moved, shifted)  6.34 us
    ppermute x4, waiting for transfers between devices, from_behind(): return lax.ppermute(block, axis, route)  5.58 us
    gather x4, local copies, waits for them, and re-layouts, shards(): extended[odd_index]  3.88 us
    gather x4, local copies, waits for them, and re-layouts, shards(): current[low_rows]  3.7 us
  transfers between devices with their start and end apart: 6, of which 6 were waited for; matrix products, arithmetic and copies ran while one was open for 3% of the time, Pallas kernels for 0%

profile of v1, /device:TPU:16, one launch (start us, length us, event | category | flops | bytes accessed | tf_op | source)
XLA Modules:
  0.0 129.0 jit_solution(1689201676267720752)
XLA Ops:
  7.2 0.9 broadcast_select_fusion
  8.2 29.5 %all-gather.3.cloned.1.call-done = f32[256,1,1,1024]{3,2,1,0:T(1,128)} async-done(((f32[64,1,1,1024]{3,2,1,0:T(1,128)}), f32[256,1,1,1024]{3,2,1,0:T(1,128)}) %all-gather.3.cloned.1.call-update) | async-done | bytes 1048592 | tf_op jit(solution)/shard_map/all_gather | solution.py:12
  37.6 1.4 %copy.11 = f32[256,1,1,1024]{3,0,1,2:T(8,128)S(1)} copy(f32[256,1,1,1024]{3,2,1,0:T(1,128)} %all-gather.3.cloned.1.call-done) | data formatting | bytes 2097152
  39.2 1.1 copy-done
  40.3 1.1 reduce.1
  41.7 2.4 %subtract_multiply_fusion = f32[64,1,4096]{2,1,0:T(1,128)} fusion(f32[64,1,4096]{2,1,0:T(1,128)S(1)} %copy-done.1, f32[64]{0:T(128)S(1)} %add_rsqrt_fusion, f32[64]{0:T(128)S(1)} %broadcast_multiply_fusion), kind=kLoop, calls=%fused_computation.35 | loop fusion | flops 524288 | bytes 2097664 | tf_op jit(solution)/shard_map/mul | solution.py:46
  44.1 10.6 %all-to-all-start = ((f32[64,1,4096]{2,1,0:T(1,128)}), f32[64,1,4096]{2,1,0:T(1,128)S(1)}, u32[]{:S(2)}, u32[]{:S(2)}) async-start(f32[64,1,4096]{2,1,0:T(1,128)} %subtract_multiply_fusion), calls=%async_computation | async-start | bytes 2097152 | tf_op jit(solution)/shard_map/all_to_all | solution.py:48
  54.9 28.7 %all-to-all-done = f32[64,1,4096]{2,1,0:T(1,128)S(1)} async-done(((f32[64,1,4096]{2,1,0:T(1,128)}), f32[64,1,4096]{2,1,0:T(1,128)S(1)}, u32[]{:S(2)}, u32[]{:S(2)}) %all-to-all-start) | async-done | bytes 1048608 | tf_op jit(solution)/shard_map/all_to_all | solution.py:48
  84.0 3.1 %collective-permute-start = (f32[32,8]{1,0:T(8,128)S(1)}, f32[32,8]{1,0:T(8,128)S(1)}, u32[]{:S(2)}, u32[]{:S(2)}) collective-permute-start(f32[32,8]{1,0:T(8,128)S(1)} %slice.201), channel_id=1, source_target_pairs={{0,1},{1,2},{2,3},{4,5},{5,6},{6,7},{8,9},{9,10},{10,11},{12,13},{... | collective-permute-start | bytes 3080 | tf_op jit(solution)/shard_map/ppermute | solution.py:18
  87.1 0.6 copy.16
  87.7 0.9 gather_fusion
  88.6 1.0 collective-permute-done
  89.8 1.0 gather_fusion.1
  92.3 0.6 reshape.759
  93.0 0.4 reshape_squeeze.13
  93.4 3.3 %collective-permute-start.1 = (f32[32,16]{1,0:T(8,128)S(1)}, f32[32,16]{1,0:T(8,128)S(1)}, u32[]{:S(2)}, u32[]{:S(2)}) collective-permute-start(f32[32,16]{1,0:T(8,128)S(1)} %slice.208), channel_id=1, source_target_pairs={{0,1},{1,2},{2,3},{4,5},{5,6},{6,7},{8,9},{9,10},{10,11},{12,13},{... | collective-permute-start | bytes 6152 | tf_op jit(solution)/shard_map/ppermute | solution.py:18
  96.7 0.9 gather_fusion.2
  97.6 1.4 %collective-permute-done.1 = f32[32,16]{1,0:T(8,128)S(1)} collective-permute-done((f32[32,16]{1,0:T(8,128)S(1)}, f32[32,16]{1,0:T(8,128)S(1)}, u32[]{:S(2)}, u32[]{:S(2)}) %collective-permute-start.1) | collective-permute-done | bytes 2080 | tf_op jit(solution)/shard_map/ppermute | solution.py:18
  99.3 1.0 gather_fusion.3
  100.2 0.4 pad_select_fusion.14
  102.7 3.1 %collective-permute-start.2 = (f32[32,32]{1,0:T(8,128)S(1)}, f32[32,32]{1,0:T(8,128)S(1)}, u32[]{:S(2)}, u32[]{:S(2)}) collective-permute-start(f32[32,32]{1,0:T(8,128)S(1)} %slice.216), channel_id=1, source_target_pairs={{0,1},{1,2},{2,3},{4,5},{5,6},{6,7},{8,9},{9,10},{10,11},{12,13},{... | collective-permute-start | bytes 12296 | tf_op jit(solution)/shard_map/ppermute | solution.py:18
  105.8 0.9 gather_fusion.4
  106.7 1.6 %collective-permute-done.2 = f32[32,32]{1,0:T(8,128)S(1)} collective-permute-done((f32[32,32]{1,0:T(8,128)S(1)}, f32[32,32]{1,0:T(8,128)S(1)}, u32[]{:S(2)}, u32[]{:S(2)}) %collective-permute-start.2) | collective-permute-done | bytes 4128 | tf_op jit(solution)/shard_map/ppermute | solution.py:18
  108.5 1.0 gather_fusion.5
  109.9 0.4 pad_select_fusion.9
  111.9 3.1 %collective-permute-start.3 = (f32[32,64]{1,0:T(8,128)S(1)}, f32[32,64]{1,0:T(8,128)S(1)}, u32[]{:S(2)}, u32[]{:S(2)}) collective-permute-start(f32[32,64]{1,0:T(8,128)S(1)} %slice.225), channel_id=1, source_target_pairs={{0,1},{1,2},{2,3},{4,5},{5,6},{6,7},{8,9},{9,10},{10,11},{12,13},{... | collective-permute-start | bytes 24584 | tf_op jit(solution)/shard_map/ppermute | solution.py:18
  114.9 0.9 gather_fusion.6
  115.9 1.6 %collective-permute-done.3 = f32[32,64]{1,0:T(8,128)S(1)} collective-permute-done((f32[32,64]{1,0:T(8,128)S(1)}, f32[32,64]{1,0:T(8,128)S(1)}, u32[]{:S(2)}, u32[]{:S(2)}) %collective-permute-start.3) | collective-permute-done | bytes 8224 | tf_op jit(solution)/shard_map/ppermute | solution.py:18
  117.7 1.0 gather_fusion.7
  119.7 0.4 pad_select_fusion.2
  120.1 0.4 pad_select_fusion.1
  120.9 1.3 %fusion = f32[64,4096]{1,0:T(8,128)} fusion(f32[64,4096]{1,0:T(8,128)S(1)} %gather_fusion.6, f32[64,4160]{1,0:T(8,128)S(1)} %pad_select_fusion, f32[64,4096]{1,0:T(8,128)S(1)} %slice.232, pred[64]{0:T(512)(128)(4,1)S(1)} %get-tuple-element.5), kind=kLoop, calls=%fused_computation.27 | loop fusion | flops 524288 | bytes 4194368 | tf_op jit(solution)/shard_map/add | solution.py:64
  (64 shorter events, 8.9 us)
Async XLA Ops:
  6.5 31.1 %all-gather.3.cloned.1.call-start = ((), (), s32[]{:S(2)}) async-start(), calls=%async_computation.1 | async-start | bytes 1310720 | tf_op jit(solution)/shard_map/all_gather | solution.py:12
  39.1 1.2 copy-start
  39.1 2.6 %copy-start.1 = (f32[64,1,4096]{2,1,0:T(1,128)S(1)}, f32[64,1,4096]{2,1,0:T(1,128)}, u32[]{:S(2)}) copy-start(f32[64,1,4096]{2,1,0:T(1,128)} %param.6) | copy-start | bytes 3145732
  44.1 10.6 %copy-start.3 = (s32[4,64]{1,0:T(4,128)S(1)}, s32[4,64]{1,0:T(4,128)}, u32[]{:S(2)}) copy-start(s32[4,64]{1,0:T(4,128)} %param.9) | copy-start | bytes 3076
  44.1 10.6 %copy-start.4 = (s32[4,64]{1,0:T(4,128)S(1)}, s32[4,64]{1,0:T(4,128)}, u32[]{:S(2)}) copy-start(s32[4,64]{1,0:T(4,128)} %param.10) | copy-start | bytes 3076
  44.1 10.7 %copy-start.2 = (s32[4,64]{1,0:T(4,128)S(1)}, s32[4,64]{1,0:T(4,128)}, u32[]{:S(2)}) copy-start(s32[4,64]{1,0:T(4,128)} %param.11) | copy-start | bytes 3076
  44.1 39.5 %all-to-all-start = ((f32[64,1,4096]{2,1,0:T(1,128)}), f32[64,1,4096]{2,1,0:T(1,128)S(1)}, u32[]{:S(2)}, u32[]{:S(2)}) async-start(f32[64,1,4096]{2,1,0:T(1,128)} %subtract_multiply_fusion), calls=%async_computation | async-start | bytes 2097152 | tf_op jit(solution)/shard_map/all_to_all | solution.py:48
  84.0 5.6 %collective-permute-start = (f32[32,8]{1,0:T(8,128)S(1)}, f32[32,8]{1,0:T(8,128)S(1)}, u32[]{:S(2)}, u32[]{:S(2)}) collective-permute-start(f32[32,8]{1,0:T(8,128)S(1)} %slice.201), channel_id=1, source_target_pairs={{0,1},{1,2},{2,3},{4,5},{5,6},{6,7},{8,9},{9,10},{10,11},{12,13},{... | collective-permute-start | bytes 3080 | tf_op jit(solution)/shard_map/ppermute | solution.py:18
  93.4 5.6 %collective-permute-start.1 = (f32[32,16]{1,0:T(8,128)S(1)}, f32[32,16]{1,0:T(8,128)S(1)}, u32[]{:S(2)}, u32[]{:S(2)}) collective-permute-start(f32[32,16]{1,0:T(8,128)S(1)} %slice.208), channel_id=1, source_target_pairs={{0,1},{1,2},{2,3},{4,5},{5,6},{6,7},{8,9},{9,10},{10,11},{12,13},{... | collective-permute-start | bytes 6152 | tf_op jit(solution)/shard_map/ppermute | solution.py:18
  102.7 5.6 %collective-permute-start.2 = (f32[32,32]{1,0:T(8,128)S(1)}, f32[32,32]{1,0:T(8,128)S(1)}, u32[]{:S(2)}, u32[]{:S(2)}) collective-permute-start(f32[32,32]{1,0:T(8,128)S(1)} %slice.216), channel_id=1, source_target_pairs={{0,1},{1,2},{2,3},{4,5},{5,6},{6,7},{8,9},{9,10},{10,11},{12,13},{... | collective-permute-start | bytes 12296 | tf_op jit(solution)/shard_map/ppermute | solution.py:18
  111.9 5.6 %collective-permute-start.3 = (f32[32,64]{1,0:T(8,128)S(1)}, f32[32,64]{1,0:T(8,128)S(1)}, u32[]{:S(2)}, u32[]{:S(2)}) collective-permute-start(f32[32,64]{1,0:T(8,128)S(1)} %slice.225), channel_id=1, source_target_pairs={{0,1},{1,2},{2,3},{4,5},{5,6},{6,7},{8,9},{9,10},{10,11},{12,13},{... | collective-permute-start | bytes 24584 | tf_op jit(solution)/shard_map/ppermute | solution.py:18
Sparse Core Ops, SparseCore 0:
  9.2 28.4 all-gather.2
